TPU v7x, 256 devices: a whole 4x4x8 slice. The times are simulated.
256 devices in a mesh: frame: 32 (over y, z_lo, x), head: 8 (over z_hi, core).
Axes of the slice: x: 4, y: 4, z: 8 (z_hi: 4, z_lo: 2; z = z_hi * 2 + z_lo), core: 2. Of those that a mesh axis runs over, the one named last changes fastest.
Arguments:
- queries: bfloat16 [65536, 2048], P(('frame', 'head')), may hold values from -32 to 32
- keys: bfloat16 [65536, 2048], P(('frame', 'head')), may hold values from -32 to 32
- values: bfloat16 [65536, 2048], P(('frame', 'head')), may hold values from -6 to 6
- windows: int32 [512, 27], P('frame'), may hold values from 0 to 511, as said below
- counts: int32 [512], replicated, may hold values from 48 to 128
Outputs:
- attended: bfloat16 [65536, 2048], P(('frame', 'head'))
Inputs may be any that keep to these rules, and one draw needn't show every extreme that they name: `windows`: row t lists tile t first, then 27 - 1 other distinct tiles whose frame pair (tile // 16) differs from that of tile t by at most one.
All inputs are finite; a program needn't handle non-finite values.
Results may differ from a plain program's by a relative error of at most 0.01.
Values may be sent and summed in bfloat16 or wider, within the bound.
A program may use at most 128 MiB of HBM per device.

v0:
```python
import jax
import jax.numpy as jnp
from jax import lax
from jax.sharding import PartitionSpec as P

HEADS = 16
HEAD_DIM = 128
TILE = 128
TL = 16


def padded(array, sides, width):
    for axis, dim in sides:
        size, length = (lax.axis_size(axis), array.shape[dim])
        up = [(i, (i + 1) % size) for i in range(size - 1)]
        down = [(j, i) for i, j in up]
        last = lax.slice_in_dim(array, length - width, length, axis=dim)
        initial = lax.slice_in_dim(array, 0, width, axis=dim)
        before = lax.ppermute(last, axis, up)
        after = lax.ppermute(initial, axis, down)
        array = jnp.concatenate([before, array, after], axis=dim)
    return array


def attend_block(query_block, key_block, value_block, usable, score_scale):
    scores = (
        jnp.einsum("tcw,tow->tco", query_block, key_block, preferred_element_type=jnp.float32)
        * score_scale
    )
    scores = jnp.where(usable[:, None, :], scores, -1e30)
    highest = jnp.max(scores, axis=-1, keepdims=True)
    attention_weights = jnp.exp(scores - highest).astype(jnp.bfloat16)
    totals = jnp.sum(attention_weights, axis=-1, keepdims=True, dtype=jnp.float32)
    mixed_values = jnp.einsum(
        "nwy,nys->nws", attention_weights, value_block, preferred_element_type=jnp.float32
    )
    return (mixed_values / totals).astype(jnp.bfloat16)


def shards(queries, keys, values, windows, counts):
    groups = lax.axis_size("head")
    local_heads = HEADS // groups
    span_tiles = windows.shape[0]
    layer_rows = TL * TILE
    frame_at = lax.axis_index("frame")
    key_value = jnp.stack([keys, values])
    q_heads, kv_local = (
        lax.all_to_all(queries[None], "head", split_axis=2, concat_axis=1, tiled=True),
        lax.all_to_all(key_value, "head", split_axis=2, concat_axis=1, tiled=True),
    )
    kv_heads = padded(kv_local, (("frame", 1),), layer_rows)
    slot_ids = windows - (frame_at * span_tiles - TL)
    columns = local_heads * HEAD_DIM
    q_tiles = q_heads[0].reshape(span_tiles, TILE, columns)
    k_tiles = kv_heads[0].reshape(-1, TILE, columns)
    v_tiles = kv_heads[1].reshape(-1, TILE, columns)
    lookup = jnp.arange(counts.shape[0], dtype=jnp.int32)
    found_counts = jnp.sum(
        jnp.where(windows[:, :, None] == lookup[None, None, :], counts[None, None, :], 0), axis=-1
    )
    usable_all = (
        jnp.arange(TILE, dtype=jnp.int32)[None, None, :] < found_counts[:, :, None]
    ).reshape(span_tiles, -1)
    block_tiles = 8
    block_count = span_tiles // block_tiles
    score_scale = HEAD_DIM ** (-0.5)

    def one_turn(counter, output):
        head_position = counter // block_count
        block_at = counter % block_count
        query_block = lax.dynamic_slice(
            q_tiles,
            (block_at * block_tiles, 0, head_position * HEAD_DIM),
            (block_tiles, TILE, HEAD_DIM),
        )
        k_head = lax.dynamic_slice_in_dim(k_tiles, head_position * HEAD_DIM, HEAD_DIM, 2)
        v_head = lax.dynamic_slice_in_dim(v_tiles, head_position * HEAD_DIM, HEAD_DIM, 2)
        picks = lax.dynamic_slice_in_dim(slot_ids, block_at * block_tiles, block_tiles, 0)
        key_block = k_head[picks].reshape(block_tiles, -1, HEAD_DIM)
        value_block = v_head[picks].reshape(block_tiles, -1, HEAD_DIM)
        usable = lax.dynamic_slice_in_dim(usable_all, block_at * block_tiles, block_tiles, 0)
        result = attend_block(query_block, key_block, value_block, usable, score_scale)
        return lax.dynamic_update_slice(
            output,
            result.reshape(block_tiles * TILE, HEAD_DIM),
            (block_at * block_tiles * TILE, head_position * HEAD_DIM),
        )

    output = lax.fori_loop(
        0,
        local_heads * block_count,
        one_turn,
        jnp.zeros((span_tiles * TILE, columns), jnp.bfloat16),
    )
    return lax.all_to_all(output, "head", split_axis=0, concat_axis=1, tiled=True)


def solution(mesh):
    in_specs = (
        P(("frame", "head"), None),
        P(("frame", "head"), None),
        P(("frame", "head"), None),
        P("frame", None),
        P(),
    )
    out_specs = P(("frame", "head"), None)
    return jax.shard_map(shards, mesh=mesh, in_specs=in_specs, out_specs=out_specs, check_vma=False)
```

profile of v0, /device:TPU:57, one launch (start us, length us, event | category | flops | bytes accessed | tf_op | source)
XLA Modules:
  0.0 392.5 jit_solution(9798144074722554429)
XLA Ops:
  3.1 4.8 %copy.31 = bf16[2,256,2048]{1,0,2:T(2,128)(2,1)S(1)} copy(bf16[2,256,2048]{2,1,0:T(8,128)(2,1)} %pad_maximum_fusion.1) | data formatting | bytes 4194304 | tf_op jit(solution)/shard_map/stack | solution.py:46
  7.9 57.7 %all_to_all.52 = bf16[2,256,2048]{1,0,2:T(2,128)(2,1)S(1)} all-to-all(bf16[2,256,2048]{1,0,2:T(2,128)(2,1)S(1)} %copy.31), channel_id=1, replica_groups=mesh['frame'=32,'head'=8] {'head'}, dimensions={2} | all-to-all | bytes 4194304 | tf_op jit(solution)/shard_map/all_to_all | solution.py:49
  71.4 4.3 %collective-permute-start.1 = (bf16[2,2048,256]{2,1,0:T(8,128)(2,1)}, bf16[2,2048,256]{2,1,0:T(8,128)(2,1)}, u32[]{:S(2)}, u32[]{:S(2)}) collective-permute-start(bf16[2,2048,256]{2,1,0:T(8,128)(2,1)} %bitcast.47), channel_id=1, source_target_pairs={{8,0},{16,8},{24,16},{32,24},{40,32},{48,40},{56,48},{64,56},{72,6... | collective-permute-start | bytes 6291464 | tf_op jit(solution)/shard_map/ppermute | solution.py:20
  77.9 10.6 %reduce = bf16[2048,256]{1,0:T(8,128)(2,1)S(1)} reduce(bf16[2048,1,256]{2,1,0:T(2,128)(2,1)S(1)} %bitcast.44, bf16[]{:T(256)} %broadcast.54), dimensions={1}, to_apply=%bitcast.25.reduce_sub_computation | reduce | bytes 2097154
  89.6 6.3 %all-to-all-start = ((bf16[8,2,32768]{2,1,0:T(2,128)(2,1)}), bf16[8,2,32768]{2,1,0:T(2,128)(2,1)S(1)}, u32[]{:S(2)}, u32[]{:S(2)}) async-start(bf16[8,2,32768]{2,1,0:T(2,128)(2,1)} %reshape.65), calls=%async_computation | async-start | bytes 2097152 | tf_op jit(solution)/shard_map/all_to_all | solution.py:48
  97.0 44.2 %all-to-all-done = bf16[8,2,32768]{2,1,0:T(2,128)(2,1)S(1)} async-done(((bf16[8,2,32768]{2,1,0:T(2,128)(2,1)}), bf16[8,2,32768]{2,1,0:T(2,128)(2,1)S(1)}, u32[]{:S(2)}, u32[]{:S(2)}) %all-to-all-start) | async-done | bytes 1048608 | tf_op jit(solution)/shard_map/all_to_all | solution.py:48
  143.7 3.9 pad_maximum_fusion
  151.7 206.2 %while.15 = (s32[]{:T(128)}, bf16[2048,256]{1,0:T(8,128)(2,1)}, pred[16,3456]{1,0:T(8,128)(4,1)S(1)}, bf16[16,128,256]{2,1,0:T(8,128)(2,1)}, bf16[48,128,256]{2,...) while((s32[]{:T(128)}, bf16[2048,256]{1,0:T(8,128)(2,1)}, ...), condition=%wide.region_4.5_spmd, body=%wide.region_1.4_spmd.sunk | while | flops 1858207360 | bytes 92443984 | solution.py:89
  153.9 8.2 %gather_fusion.1 = bf16[216,128,128]{2,1,0:T(8,128)(2,1)} fusion(bf16[48,128,128]{2,1,0:T(8,128)(2,1)S(1)} %get-tuple-element.254, s32[1024]{0:T(1024)S(1)} %pad_clamp_fusion.2), kind=kCustom, calls=%fused_computation.clone.1 | custom fusion | bytes 14156640 | tf_op jit(solution)/shard_map/while/body/eval_jaxpr/gather | solution.py:79
  162.1 10.5 %fusion.16 = (f32[8,128]{1,0:T(8,128)S(1)}, f32[8,128,3456]{2,1,0:T(8,128)}) fusion(pred[8,3456]{1,0:T(8,128)(4,1)S(1)} %constant_dynamic-slice_fusion.6, bf16[8,3456,128]{2,1,0:T(8,128)(2,1)} %bitcast.39, bf16[16,128,256]{2,1,0:T(8,128)(2,1)} %get-tuple-element.294, s32[]{:T(128)S(6)} %select_n.120, s32[]{:T(128)S(6)} %select_n.118), kind=kOutput, calls=%fused_computation.5.clone.1 | convolution fusion | flops 916585472 | bytes 21527560 | tf_op jit(solution)/shard_map/while/body/eval_jaxpr/tcw,tow->tco/dot_general | solution.py:27
  172.6 8.3 %convert_reduce_fusion.2 = f32[8,128]{1,0:T(8,128)S(1)} fusion(f32[8,128]{1,0:T(8,128)S(1)} %get-tuple-element.255, f32[8,128,3456]{2,1,0:T(8,128)} %get-tuple-element.256, pred[8,3456]{1,0:T(8,128)(4,1)S(1)} %constant_dynamic-slice_fusion.6), kind=kLoop, calls=%fused_computation.2.clone.1 | loop fusion | flops 21232640 | bytes 14191616 | tf_op jit(solution)/shard_map/while/body/eval_jaxpr/reduce_sum | solution.py:33
  180.9 8.2 %gather_fusion = bf16[216,128,128]{2,1,0:T(8,128)(2,1)} fusion(bf16[48,128,128]{2,1,0:T(8,128)(2,1)S(1)} %get-tuple-element.253, s32[1024]{0:T(1024)S(1)} %pad_clamp_fusion.2), kind=kCustom, calls=%fused_computation.1.clone.1 | custom fusion | bytes 14156640 | tf_op jit(solution)/shard_map/while/body/eval_jaxpr/gather | solution.py:80
  189.1 10.3 %fusion.17 = bf16[8,128,128]{2,1,0:T(8,128)(2,1)S(1)} fusion(bf16[8,3456,128]{2,1,0:T(8,128)(2,1)} %bitcast.40, f32[8,128]{1,0:T(8,128)S(1)} %convert_reduce_fusion.2, f32[8,128,3456]{2,1,0:T(8,128)} %get-tuple-element.256, f32[8,128]{1,0:T(8,128)S(1)} %get-tuple-element.255, pred[8,3456]{1,0:T(8,128)(4,1)S(1)} %constant_dynamic-slice_fusion.6), kind=kOutput, calls=%fused_computation.7.clone.1 | convolution fusion | flops 920387584 | bytes 21531648 | tf_op jit(solution)/shard_map/while/body/eval_jaxpr/nwy,nys->nws/dot_general | solution.py:34
  199.4 4.6 %dynamic_update_slice.11 = bf16[2048,256]{1,0:T(8,128)(2,1)} dynamic-update-slice(bf16[2048,256]{1,0:T(8,128)(2,1)} %get-tuple-element.275, bf16[1024,128]{1,0:T(8,128)(2,1)S(1)} %bitcast.49, s32[]{:T(128)S(6)} %select_n.121, s32[]{:T(128)S(6)} %select_n.118) | dynamic-update-slice | bytes 524292 | tf_op jit(solution)/shard_map/while/body/eval_jaxpr/dynamic_update_slice | solution.py:83
  206.2 8.2 %gather_fusion.1 = bf16[216,128,128]{2,1,0:T(8,128)(2,1)} fusion(bf16[48,128,128]{2,1,0:T(8,128)(2,1)S(1)} %get-tuple-element.254, s32[1024]{0:T(1024)S(1)} %pad_clamp_fusion.2), kind=kCustom, calls=%fused_computation.clone.1 | custom fusion | bytes 14156640 | tf_op jit(solution)/shard_map/while/body/eval_jaxpr/gather | solution.py:79
  214.4 10.5 %fusion.16 = (f32[8,128]{1,0:T(8,128)S(1)}, f32[8,128,3456]{2,1,0:T(8,128)}) fusion(pred[8,3456]{1,0:T(8,128)(4,1)S(1)} %constant_dynamic-slice_fusion.6, bf16[8,3456,128]{2,1,0:T(8,128)(2,1)} %bitcast.39, bf16[16,128,256]{2,1,0:T(8,128)(2,1)} %get-tuple-element.294, s32[]{:T(128)S(6)} %select_n.120, s32[]{:T(128)S(6)} %select_n.118), kind=kOutput, calls=%fused_computation.5.clone.1 | convolution fusion | flops 916585472 | bytes 21527560 | tf_op jit(solution)/shard_map/while/body/eval_jaxpr/tcw,tow->tco/dot_general | solution.py:27
  224.9 8.3 %convert_reduce_fusion.2 = f32[8,128]{1,0:T(8,128)S(1)} fusion(f32[8,128]{1,0:T(8,128)S(1)} %get-tuple-element.255, f32[8,128,3456]{2,1,0:T(8,128)} %get-tuple-element.256, pred[8,3456]{1,0:T(8,128)(4,1)S(1)} %constant_dynamic-slice_fusion.6), kind=kLoop, calls=%fused_computation.2.clone.1 | loop fusion | flops 21232640 | bytes 14191616 | tf_op jit(solution)/shard_map/while/body/eval_jaxpr/reduce_sum | solution.py:33
  233.2 8.2 %gather_fusion = bf16[216,128,128]{2,1,0:T(8,128)(2,1)} fusion(bf16[48,128,128]{2,1,0:T(8,128)(2,1)S(1)} %get-tuple-element.253, s32[1024]{0:T(1024)S(1)} %pad_clamp_fusion.2), kind=kCustom, calls=%fused_computation.1.clone.1 | custom fusion | bytes 14156640 | tf_op jit(solution)/shard_map/while/body/eval_jaxpr/gather | solution.py:80
  241.4 10.3 %fusion.17 = bf16[8,128,128]{2,1,0:T(8,128)(2,1)S(1)} fusion(bf16[8,3456,128]{2,1,0:T(8,128)(2,1)} %bitcast.40, f32[8,128]{1,0:T(8,128)S(1)} %convert_reduce_fusion.2, f32[8,128,3456]{2,1,0:T(8,128)} %get-tuple-element.256, f32[8,128]{1,0:T(8,128)S(1)} %get-tuple-element.255, pred[8,3456]{1,0:T(8,128)(4,1)S(1)} %constant_dynamic-slice_fusion.6), kind=kOutput, calls=%fused_computation.7.clone.1 | convolution fusion | flops 920387584 | bytes 21531648 | tf_op jit(solution)/shard_map/while/body/eval_jaxpr/nwy,nys->nws/dot_general | solution.py:34
  251.7 3.6 dynamic_update_slice.11
  257.6 8.2 %gather_fusion.1 = bf16[216,128,128]{2,1,0:T(8,128)(2,1)} fusion(bf16[48,128,128]{2,1,0:T(8,128)(2,1)S(1)} %get-tuple-element.254, s32[1024]{0:T(1024)S(1)} %pad_clamp_fusion.2), kind=kCustom, calls=%fused_computation.clone.1 | custom fusion | bytes 14156640 | tf_op jit(solution)/shard_map/while/body/eval_jaxpr/gather | solution.py:79
  265.8 10.5 %fusion.16 = (f32[8,128]{1,0:T(8,128)S(1)}, f32[8,128,3456]{2,1,0:T(8,128)}) fusion(pred[8,3456]{1,0:T(8,128)(4,1)S(1)} %constant_dynamic-slice_fusion.6, bf16[8,3456,128]{2,1,0:T(8,128)(2,1)} %bitcast.39, bf16[16,128,256]{2,1,0:T(8,128)(2,1)} %get-tuple-element.294, s32[]{:T(128)S(6)} %select_n.120, s32[]{:T(128)S(6)} %select_n.118), kind=kOutput, calls=%fused_computation.5.clone.1 | convolution fusion | flops 916585472 | bytes 21527560 | tf_op jit(solution)/shard_map/while/body/eval_jaxpr/tcw,tow->tco/dot_general | solution.py:27
  276.2 8.3 %convert_reduce_fusion.2 = f32[8,128]{1,0:T(8,128)S(1)} fusion(f32[8,128]{1,0:T(8,128)S(1)} %get-tuple-element.255, f32[8,128,3456]{2,1,0:T(8,128)} %get-tuple-element.256, pred[8,3456]{1,0:T(8,128)(4,1)S(1)} %constant_dynamic-slice_fusion.6), kind=kLoop, calls=%fused_computation.2.clone.1 | loop fusion | flops 21232640 | bytes 14191616 | tf_op jit(solution)/shard_map/while/body/eval_jaxpr/reduce_sum | solution.py:33
  284.6 8.2 %gather_fusion = bf16[216,128,128]{2,1,0:T(8,128)(2,1)} fusion(bf16[48,128,128]{2,1,0:T(8,128)(2,1)S(1)} %get-tuple-element.253, s32[1024]{0:T(1024)S(1)} %pad_clamp_fusion.2), kind=kCustom, calls=%fused_computation.1.clone.1 | custom fusion | bytes 14156640 | tf_op jit(solution)/shard_map/while/body/eval_jaxpr/gather | solution.py:80
  292.8 10.3 %fusion.17 = bf16[8,128,128]{2,1,0:T(8,128)(2,1)S(1)} fusion(bf16[8,3456,128]{2,1,0:T(8,128)(2,1)} %bitcast.40, f32[8,128]{1,0:T(8,128)S(1)} %convert_reduce_fusion.2, f32[8,128,3456]{2,1,0:T(8,128)} %get-tuple-element.256, f32[8,128]{1,0:T(8,128)S(1)} %get-tuple-element.255, pred[8,3456]{1,0:T(8,128)(4,1)S(1)} %constant_dynamic-slice_fusion.6), kind=kOutput, calls=%fused_computation.7.clone.1 | convolution fusion | flops 920387584 | bytes 21531648 | tf_op jit(solution)/shard_map/while/body/eval_jaxpr/nwy,nys->nws/dot_general | solution.py:34
  303.1 3.9 %dynamic_update_slice.11 = bf16[2048,256]{1,0:T(8,128)(2,1)} dynamic-update-slice(bf16[2048,256]{1,0:T(8,128)(2,1)} %get-tuple-element.275, bf16[1024,128]{1,0:T(8,128)(2,1)S(1)} %bitcast.49, s32[]{:T(128)S(6)} %select_n.121, s32[]{:T(128)S(6)} %select_n.118) | dynamic-update-slice | bytes 524292 | tf_op jit(solution)/shard_map/while/body/eval_jaxpr/dynamic_update_slice | solution.py:83
  309.2 8.2 %gather_fusion.1 = bf16[216,128,128]{2,1,0:T(8,128)(2,1)} fusion(bf16[48,128,128]{2,1,0:T(8,128)(2,1)S(1)} %get-tuple-element.254, s32[1024]{0:T(1024)S(1)} %pad_clamp_fusion.2), kind=kCustom, calls=%fused_computation.clone.1 | custom fusion | bytes 14156640 | tf_op jit(solution)/shard_map/while/body/eval_jaxpr/gather | solution.py:79
  317.4 10.5 %fusion.16 = (f32[8,128]{1,0:T(8,128)S(1)}, f32[8,128,3456]{2,1,0:T(8,128)}) fusion(pred[8,3456]{1,0:T(8,128)(4,1)S(1)} %constant_dynamic-slice_fusion.6, bf16[8,3456,128]{2,1,0:T(8,128)(2,1)} %bitcast.39, bf16[16,128,256]{2,1,0:T(8,128)(2,1)} %get-tuple-element.294, s32[]{:T(128)S(6)} %select_n.120, s32[]{:T(128)S(6)} %select_n.118), kind=kOutput, calls=%fused_computation.5.clone.1 | convolution fusion | flops 916585472 | bytes 21527560 | tf_op jit(solution)/shard_map/while/body/eval_jaxpr/tcw,tow->tco/dot_general | solution.py:27
  327.9 8.3 %convert_reduce_fusion.2 = f32[8,128]{1,0:T(8,128)S(1)} fusion(f32[8,128]{1,0:T(8,128)S(1)} %get-tuple-element.255, f32[8,128,3456]{2,1,0:T(8,128)} %get-tuple-element.256, pred[8,3456]{1,0:T(8,128)(4,1)S(1)} %constant_dynamic-slice_fusion.6), kind=kLoop, calls=%fused_computation.2.clone.1 | loop fusion | flops 21232640 | bytes 14191616 | tf_op jit(solution)/shard_map/while/body/eval_jaxpr/reduce_sum | solution.py:33
  336.2 8.2 %gather_fusion = bf16[216,128,128]{2,1,0:T(8,128)(2,1)} fusion(bf16[48,128,128]{2,1,0:T(8,128)(2,1)S(1)} %get-tuple-element.253, s32[1024]{0:T(1024)S(1)} %pad_clamp_fusion.2), kind=kCustom, calls=%fused_computation.1.clone.1 | custom fusion | bytes 14156640 | tf_op jit(solution)/shard_map/while/body/eval_jaxpr/gather | solution.py:80
  344.4 10.3 %fusion.17 = bf16[8,128,128]{2,1,0:T(8,128)(2,1)S(1)} fusion(bf16[8,3456,128]{2,1,0:T(8,128)(2,1)} %bitcast.40, f32[8,128]{1,0:T(8,128)S(1)} %convert_reduce_fusion.2, f32[8,128,3456]{2,1,0:T(8,128)} %get-tuple-element.256, f32[8,128]{1,0:T(8,128)S(1)} %get-tuple-element.255, pred[8,3456]{1,0:T(8,128)(4,1)S(1)} %constant_dynamic-slice_fusion.6), kind=kOutput, calls=%fused_computation.7.clone.1 | convolution fusion | flops 920387584 | bytes 21531648 | tf_op jit(solution)/shard_map/while/body/eval_jaxpr/nwy,nys->nws/dot_general | solution.py:34
  357.9 32.6 %all_to_all.53 = bf16[8,256,256]{2,1,0:T(8,128)(2,1)S(1)} all-to-all(bf16[8,256,256]{2,1,0:T(8,128)(2,1)} %bitcast.52), channel_id=1, replica_groups=mesh['frame'=32,'head'=8] {'head'}, dimensions={0} | all-to-all | bytes 2097152 | tf_op jit(solution)/shard_map/all_to_all | solution.py:95
  (50 shorter events, 33.8 us)
Async XLA Ops:
  7.9 67.8 %copy-start = (bf16[256,2048]{1,0:T(8,128)(2,1)S(1)}, bf16[256,2048]{1,0:T(8,128)(2,1)}, u32[]{:S(2)}) copy-start(bf16[256,2048]{1,0:T(8,128)(2,1)} %param.7) | copy-start | bytes 3145732
  65.9 30.0 %copy-start.1 = (s32[16,27]{1,0:T(8,128)S(1)}, s32[16,27]{1,0:T(8,128)}, u32[]{:S(2)}) copy-start(s32[16,27]{1,0:T(8,128)} %param.10) | copy-start | bytes 5188
  65.9 30.1 %copy-start.2 = (s32[512]{0:T(512)S(1)}, s32[512]{0:T(512)}, u32[]{:S(2)}) copy-start(s32[512]{0:T(512)} %param.11) | copy-start | bytes 6148
  68.3 75.4 %collective-permute-start = (bf16[2,2048,256]{2,1,0:T(8,128)(2,1)}, bf16[2,2048,256]{2,1,0:T(8,128)(2,1)}, u32[]{:S(2)}, u32[]{:S(2)}) collective-permute-start(bf16[2,2048,256]{2,1,0:T(8,128)(2,1)} %bitcast.46), channel_id=1, source_target_pairs={{0,8},{8,16},{16,24},{24,32},{32,40},{40,48},{48,56},{56,64},{64,7... | collective-permute-start | bytes 6291464 | tf_op jit(solution)/shard_map/ppermute | solution.py:19
  71.4 72.3 %collective-permute-start.1 = (bf16[2,2048,256]{2,1,0:T(8,128)(2,1)}, bf16[2,2048,256]{2,1,0:T(8,128)(2,1)}, u32[]{:S(2)}, u32[]{:S(2)}) collective-permute-start(bf16[2,2048,256]{2,1,0:T(8,128)(2,1)} %bitcast.47), channel_id=1, source_target_pairs={{8,0},{16,8},{24,16},{32,24},{40,32},{48,40},{56,48},{64,56},{72,6... | collective-permute-start | bytes 6291464 | tf_op jit(solution)/shard_map/ppermute | solution.py:20
  89.6 51.6 %all-to-all-start = ((bf16[8,2,32768]{2,1,0:T(2,128)(2,1)}), bf16[8,2,32768]{2,1,0:T(2,128)(2,1)S(1)}, u32[]{:S(2)}, u32[]{:S(2)}) async-start(bf16[8,2,32768]{2,1,0:T(2,128)(2,1)} %reshape.65), calls=%async_computation | async-start | bytes 2097152 | tf_op jit(solution)/shard_map/all_to_all | solution.py:48
where the time goes:
time: 400 us; the launch traced here: 392 us
  local copies, waits for them, and re-layouts  109 us (27%)
  blocking collectives  90.2 us (23%)
  matrix products  83.1 us (21%)
  other arithmetic  51.7 us (13%)
  waiting for transfers between devices  44.2 us (11%)
  starting transfers between devices  13.6 us (3%)
    all_to_all x1, blocking collectives, shards(): lax.all_to_all(key_value, 'head', split_axis=2, concat_axis=1, tiled=True)  57.7 us
    all_to_all x1, waiting for transfers between devices, shards(): lax.all_to_all(queries[None], 'head', split_axis=2, concat_axis=1, tiled=...  44.2 us
    dot_general x4, matrix products, attend_block(): jnp.einsum('tcw,tow->tco', query_block, key_block, preferred_element_type...  41.9 us
    dot_general x4, matrix products, attend_block(): jnp.einsum('nwy,nys->nws', attention_weights, value_block, preferred_elem...  41.3 us
    reduce_sum x4, other arithmetic, attend_block(): jnp.sum(attention_weights, axis=-1, keepdims=True, dtype=jnp.float32)  33.3 us
    gather x4, local copies, waits for them, and re-layouts, one_turn(): key_block = k_head[picks].reshape(block_tiles, -1, HEAD_DIM)  32.8 us
    gather x4, local copies, waits for them, and re-layouts, one_turn(): value_block = v_head[picks].reshape(block_tiles, -1, HEAD_DIM)  32.8 us
    all_to_all x1, blocking collectives, shards(): lax.all_to_all(output, 'head', split_axis=0, concat_axis=1, tiled=True)  32.6 us
  transfers between devices with their start and end apart: 3, of which 1 were waited for; matrix products, arithmetic and copies ran while one was open for 4% of the time, Pallas kernels for 0%

commit v1 on v0

v1 whole, which is shorter than its diff:
```python
import math

import jax
import jax.numpy as jnp
from jax import lax
from jax.experimental import pallas as pl
from jax.experimental.pallas import tpu as pltpu
from jax.sharding import PartitionSpec as P

HEADS = 16
DIM = 128
TILE = 128
WIN = 27
TL = 16
PEERS = 16
ROWS = 256
SCALE = math.log2(math.e) / math.sqrt(DIM)
MESH = pl.DeviceIdType.MESH


def div(a, b):
    return lax.div(a, jnp.int32(b))


def rem(a, b):
    return lax.rem(a, jnp.int32(b))


def owner(pair, head):
    z, b = div(head, 2), rem(head, 2)
    zh = div(z, 2)
    x = 2 * b + rem(div(pair, 2) + div(pair, 4) + zh, 2)
    return (div(pair, 4) * 2 + rem(z, 2)) * 4 + x, zh * 2 + rem(pair, 2)


def spread(k):
    return div(k + 1, 2) * (2 * rem(k, 2) - 1)


def kernel(
    q_ref, k_ref, v_ref, win_ref, counts_hbm, out_ref,
    qbuf, kraw, vraw, keys, vals, obuf, scores, wdst, wsm, counts_ref,
    in_send, in_recv, halo_send, halo_recv, o_send, o_recv, w_send, w_recv, local,
):
    f, hi = lax.axis_index("frame"), lax.axis_index("head")
    zl, x = rem(div(f, 4), 2), rem(f, 4)
    zh, core = div(hi, 2), rem(hi, 2)
    src_pair = div(f, 2)
    my_slot = rem(f, 2) * 8 + hi
    my_z = zh * 2 + zl
    head = 2 * my_z + div(x, 2)
    pair = div(f, 8) * 4 + rem(x + zh + div(f, 8), 2) * 2 + core
    last_pair = lax.axis_size("frame") // 2 - 1
    has_left, has_right = pair > 0, pair < last_pair
    left = owner(jnp.maximum(pair - 1, 0), head)
    right = owner(jnp.minimum(pair + 1, last_pair), head)

    def is_me(dev):
        return (dev[0] == f) & (dev[1] == hi)

    sign = 1 - 2 * core

    def dest_head(i, side):
        z = rem(my_z + side * spread(div(i, 2)) + 8, 8)
        return 2 * z + rem(i, 2)

    def source_slot(i):
        r = rem(i, 4)
        z = rem(zh + sign * spread(div(i, 4)) + 4, 4)
        return rem(r, 2) * 8 + z * 2 + div(r, 2)

    def source_dev(slot):
        return 2 * pair + div(slot, 8), rem(slot, 8)

    barrier = pltpu.get_barrier_semaphore()

    def greet(dev, when):
        @pl.when(when)
        def _():
            pl.semaphore_signal(barrier, inc=1, device_id=dev, device_id_type=MESH)

    def greet_step(i, carry):
        src = source_dev(i)
        greet(src, jnp.logical_not(is_me(src)))
        return carry

    counts_copy = pltpu.make_async_copy(counts_hbm, counts_ref, local.at[0])
    counts_copy.start()
    lax.fori_loop(0, PEERS, greet_step, 0)
    greet(left, has_left)
    greet(right, has_right)
    selfish = (div(f, 2) == pair).astype(jnp.int32)
    pl.semaphore_wait(
        barrier, 16 - selfish + has_left.astype(jnp.int32) + has_right.astype(jnp.int32)
    )

    def send(a, src_ref, dst_ref, h):
        dst = owner(src_pair, h)
        src = src_ref.at[:, pl.ds(pl.multiple_of(h * DIM, DIM), DIM)]
        mine = is_me(dst)

        @pl.when(jnp.logical_not(mine))
        def _():
            pltpu.make_async_remote_copy(
                src_ref=src, dst_ref=dst_ref, send_sem=in_send.at[a, h],
                recv_sem=in_recv.at[a, my_slot], device_id=dst, device_id_type=MESH,
            ).start()

        @pl.when(mine)
        def _():
            pltpu.make_async_copy(src, dst_ref, in_recv.at[a, my_slot]).start()

    def sends(i, carry):
        send(0, k_ref, kraw.at[8 + my_slot], dest_head(i, sign))
        send(1, v_ref, vraw.at[8 + my_slot], dest_head(i, -sign))
        return carry

    def window_send(b, start):
        h = 2 * hi + b
        dst = owner(src_pair, h)
        mine = is_me(dst)
        there = wdst.at[rem(f, 2)]

        @pl.when(jnp.logical_not(mine))
        def _():
            copy = pltpu.make_async_remote_copy(
                src_ref=win_ref, dst_ref=there, send_sem=w_send.at[b],
                recv_sem=w_recv.at[rem(f, 2)], device_id=dst, device_id_type=MESH,
            )
            if start:
                copy.start()
            else:
                copy.wait_send()

        if start:

            @pl.when(mine)
            def _():
                pltpu.make_async_copy(win_ref, there, w_recv.at[rem(f, 2)]).start()

    for b in range(2):
        window_send(b, True)
    lax.fori_loop(0, PEERS, sends, 0)

    first_tile = (2 * pair - 1) * TL
    row_ids = lax.broadcasted_iota(jnp.int32, (TILE, DIM), 0)

    def prepare(r):
        for u in range(2):
            count = counts_ref[first_tile + 2 * r + u]
            usable = row_ids < count
            k = kraw[r, u * TILE : (u + 1) * TILE, :].astype(jnp.float32)
            keys[2 * r + u] = jnp.where(usable, k, k[0:1, :]).astype(jnp.bfloat16)
            v = vraw[r, u * TILE : (u + 1) * TILE, :].astype(jnp.float32)
            vals[2 * r + u, :, 0:DIM] = jnp.where(usable, v, 0.0).astype(jnp.bfloat16)
            vals[2 * r + u, :, DIM : 2 * DIM] = jnp.where(usable, 1.0, 0.0).astype(jnp.bfloat16)

    def halo(a, raw, slot, dev, there):
        return pltpu.make_async_remote_copy(
            src_ref=raw.at[8 + slot], dst_ref=raw.at[there], send_sem=halo_send.at[a, slot],
            recv_sem=halo_recv.at[a, slot], device_id=dev, device_id_type=MESH,
        )

    def arrivals(i, carry):
        slot = source_slot(i)
        for a, raw in ((0, kraw), (1, vraw)):
            here = raw.at[8 + slot]
            pltpu.make_async_copy(here, here, in_recv.at[a, slot]).wait()

            @pl.when((slot < 8) & has_left)
            def _():
                halo(a, raw, slot, left, 24 + rem(slot, 8)).start()

            @pl.when((slot >= 8) & has_right)
            def _():
                halo(a, raw, slot, right, rem(slot, 8)).start()

        send(2, q_ref, qbuf.at[my_slot], dest_head(i, sign))
        prepare(8 + slot)
        return carry

    counts_copy.wait()
    lax.fori_loop(0, PEERS, arrivals, 0)

    def halo_arrivals(i, carry):
        slot = source_slot(i)
        from_left = slot >= 8
        r = lax.select(from_left, rem(slot, 8), 24 + rem(slot, 8))

        @pl.when((from_left & has_left) | (jnp.logical_not(from_left) & has_right))
        def _():
            for a, raw in ((0, kraw), (1, vraw)):
                here = raw.at[r]
                pltpu.make_async_copy(here, here, halo_recv.at[a, slot]).wait()
            prepare(r)

        return carry

    for half in range(2):
        here = wdst.at[half]
        pltpu.make_async_copy(here, here, w_recv.at[half]).wait()
    copy = pltpu.make_async_copy(wdst, wsm, local.at[1])
    copy.start()
    copy.wait()
    lax.fori_loop(0, PEERS, halo_arrivals, 0)

    def attend(slot, u):
        q = qbuf[slot, u * TILE : (u + 1) * TILE, :]
        half, row = div(slot, 8), 2 * rem(slot, 8) + u
        at = [jnp.clip(wsm[half, row, j] - first_tile, 0, 4 * TL - 1) for j in range(WIN)]
        highest = None
        for j in range(0, WIN, 2):
            k = keys[at[j]]
            if j + 1 < WIN:
                k = jnp.concatenate([k, keys[at[j + 1]]], axis=0)
            s = lax.dot_general(q, k, (((1,), (1,)), ((), ())), preferred_element_type=jnp.float32)
            scores[u, :, j * TILE : j * TILE + k.shape[0]] = s
            for part in range(k.shape[0] // TILE):
                block = s[:, part * TILE : (part + 1) * TILE]
                highest = block if highest is None else jnp.maximum(highest, block)
        highest = jnp.max(highest, axis=1, keepdims=True)
        total = jnp.zeros((TILE, 2 * DIM), jnp.float32)
        for j in range(0, WIN, 2):
            v = vals[at[j]]
            if j + 1 < WIN:
                v = jnp.concatenate([v, vals[at[j + 1]]], axis=0)
            s = scores[u, :, j * TILE : j * TILE + v.shape[0]]
            weights = jnp.exp2((s - highest) * SCALE).astype(jnp.bfloat16)
            total += jnp.dot(weights, v, preferred_element_type=jnp.float32)
        result = total[:, :DIM] / total[:, DIM:]
        obuf[slot, u * TILE : (u + 1) * TILE, :] = result.astype(jnp.bfloat16)

    columns = pl.ds(pl.multiple_of(head * DIM, DIM), DIM)

    def result_copy(slot, dev):
        return pltpu.make_async_remote_copy(
            src_ref=obuf.at[slot], dst_ref=out_ref.at[:, columns], send_sem=o_send.at[slot],
            recv_sem=o_recv.at[head], device_id=dev, device_id_type=MESH,
        )

    def compute(i, carry):
        slot = source_slot(i)
        here = qbuf.at[slot]
        pltpu.make_async_copy(here, here, in_recv.at[2, slot]).wait()
        for u in range(2):
            attend(slot, u)
        dev = source_dev(slot)
        mine = is_me(dev)

        @pl.when(jnp.logical_not(mine))
        def _():
            result_copy(slot, dev).start()

        @pl.when(mine)
        def _():
            pltpu.make_async_copy(obuf.at[slot], out_ref.at[:, columns], o_recv.at[head]).start()

        return carry

    lax.fori_loop(0, PEERS, compute, 0)

    def finish(i, carry):
        dst = owner(src_pair, i)

        @pl.when(jnp.logical_not(is_me(dst)))
        def _():
            for a, ref in ((0, k_ref), (1, v_ref), (2, q_ref)):
                src = ref.at[:, pl.ds(pl.multiple_of(i * DIM, DIM), DIM)]
                pltpu.make_async_copy(src, src, in_send.at[a, i]).wait()

        @pl.when(((i < 8) & has_left) | ((i >= 8) & has_right))
        def _():
            for a, raw in ((0, kraw), (1, vraw)):
                there = raw.at[8 + i]
                pltpu.make_async_copy(there, there, halo_send.at[a, i]).wait()

        @pl.when(jnp.logical_not(is_me(source_dev(i))))
        def _():
            pltpu.make_async_copy(obuf.at[i], obuf.at[i], o_send.at[i]).wait()

        got = out_ref.at[:, pl.ds(pl.multiple_of(i * DIM, DIM), DIM)]
        pltpu.make_async_copy(got, got, o_recv.at[i]).wait()
        return carry

    lax.fori_loop(0, PEERS, finish, 0)
    for b in range(2):
        window_send(b, False)


def shards(queries, keys, values, windows, counts):
    anywhere = pl.BlockSpec(memory_space=pltpu.HBM)
    dma = pltpu.SemaphoreType.DMA
    return pl.pallas_call(
        kernel,
        out_shape=jax.ShapeDtypeStruct(queries.shape, jnp.bfloat16),
        in_specs=[
            anywhere,
            anywhere,
            anywhere,
            anywhere,
            anywhere,
        ],
        out_specs=anywhere,
        scratch_shapes=[
            pltpu.VMEM((PEERS, ROWS, DIM), jnp.bfloat16),
            pltpu.VMEM((2 * PEERS, ROWS, DIM), jnp.bfloat16),
            pltpu.VMEM((2 * PEERS, ROWS, DIM), jnp.bfloat16),
            pltpu.VMEM((4 * TL, TILE, DIM), jnp.bfloat16),
            pltpu.VMEM((4 * TL, TILE, 2 * DIM), jnp.bfloat16),
            pltpu.VMEM((PEERS, ROWS, DIM), jnp.bfloat16),
            pltpu.VMEM((2, TILE, WIN * TILE), jnp.float32),
            pltpu.VMEM((2, TL, WIN), jnp.int32),
            pltpu.SMEM((2, TL, WIN), jnp.int32),
            pltpu.SMEM((32 * TL,), jnp.int32),
            dma((3, PEERS)),
            dma((3, PEERS)),
            dma((2, PEERS)),
            dma((2, PEERS)),
            dma((PEERS,)),
            dma((PEERS,)),
            dma((2,)),
            dma((2,)),
            dma((2,)),
        ],
        compiler_params=pltpu.CompilerParams(
            collective_id=0, has_side_effects=True, vmem_limit_bytes=48 * 1024 * 1024
        ),
        name="tile_attention",
    )(queries, keys, values, windows, counts)


def solution(mesh):
    tokens = P(("frame", "head"), None)
    return jax.shard_map(
        shards,
        mesh=mesh,
        in_specs=(tokens, tokens, tokens, P("frame", None), P()),
        out_specs=tokens,
        check_vma=False,
    )
```

time: 400 us -> 121 us (0.30); the launches traced: 392 us -> 119 us
  Pallas kernels: 0 us -> 113 us
  local copies, waits for them, and re-layouts: 109 us -> 6.02 us
  blocking collectives: 90.2 us -> 0 us
  matrix products: 83.1 us -> 0 us
  other arithmetic: 51.7 us -> 0 us
  waiting for transfers between devices: 44.2 us -> 0 us
  starting transfers between devices: 13.6 us -> 0 us
    pallas_call x0 -> x1, Pallas kernels: none -> 113 us  [shards(): pl.pallas_call(kernel, out_shape=jax.ShapeDtypeStruct(queries.shape, jnp....]
    all_to_all x2 -> x0, blocking collectives: 90.2 us -> none  [the longest x1 57.7 us: shards(): lax.all_to_all(key_value, 'head', split_axis=2, concat_axis=1, tiled=True)]
    dot_general x8 -> x0, matrix products: 83.1 us -> none  [the longest x4 41.9 us: attend_block(): jnp.einsum('tcw,tow->tco', query_block, key_block, preferred_element_type...]
    gather x8 -> x0, local copies, waits for them, and re-layouts: 65.6 us -> none  [the longest x4 32.8 us: one_turn(): key_block = k_head[picks].reshape(block_tiles, -1, HEAD_DIM)]
    all_to_all x1 -> x0, waiting for transfers between devices: 44.2 us -> none  [shards(): lax.all_to_all(queries[None], 'head', split_axis=2, concat_axis=1, tiled=...]
    reduce_sum x5 -> x0, other arithmetic: 33.9 us -> none  [the longest x4 33.3 us: attend_block(): jnp.sum(attention_weights, axis=-1, keepdims=True, dtype=jnp.float32)]
    dynamic_update_slice x4 -> x0, local copies, waits for them, and re-layouts: 15.3 us -> none  [one_turn(): lax.dynamic_update_slice(output, result.reshape(block_tiles * TILE, HEAD_...]
    unnamed x1 -> x0, other arithmetic: 10.6 us -> none
  transfers between devices with their start and end apart: 3 -> 0, of which waited for: 1 -> 0; matrix products, arithmetic and copies ran while one was open for 4% -> 0% of each run, Pallas kernels for 0% -> 0%
where the time goes in v1:
time: 121 us; the launch traced here: 119 us
  Pallas kernels  113 us (93%)
  local copies, waits for them, and re-layouts  6.02 us (5%)
    pallas_call x1, Pallas kernels, shards(): pl.pallas_call(kernel, out_shape=jax.ShapeDtypeStruct(queries.shape, jnp....  113 us
    unnamed x11, local copies, waits for them, and re-layouts  6.02 us

profile of v1, /device:TPU:57, one launch (start us, length us, event | category | flops | bytes accessed | tf_op | source)
XLA Modules:
  0.0 118.7 jit_solution(17765225116834190302)
XLA Ops:
  0.0 0.0 copy-start
  0.0 1.2 %copy-done = bf16[256,2048]{1,0:T(8,128)(2,1)S(1)} copy-done((bf16[256,2048]{1,0:T(8,128)(2,1)S(1)}, bf16[256,2048]{1,0:T(8,128)(2,1)}, u32[]{:S(2)}) %copy-start) | copy-done | bytes 1048600
  1.2 0.0 copy-start.1
  1.2 1.2 %copy-done.1 = bf16[256,2048]{1,0:T(8,128)(2,1)S(1)} copy-done((bf16[256,2048]{1,0:T(8,128)(2,1)S(1)}, bf16[256,2048]{1,0:T(8,128)(2,1)}, u32[]{:S(2)}) %copy-start.1) | copy-done | bytes 1048600
  2.5 0.0 copy-start.2
  2.5 1.2 %copy-done.2 = bf16[256,2048]{1,0:T(8,128)(2,1)S(1)} copy-done((bf16[256,2048]{1,0:T(8,128)(2,1)S(1)}, bf16[256,2048]{1,0:T(8,128)(2,1)}, u32[]{:S(2)}) %copy-start.2) | copy-done | bytes 1048600
  3.7 0.0 copy-start.3
  3.7 0.7 copy-done.3
  4.4 0.0 copy-start.4
  4.4 0.7 copy-done.4
  5.1 112.7 %tile_attention.1 = bf16[256,2048]{1,0:T(8,128)(2,1)S(1)} custom-call(bf16[256,2048]{1,0:T(8,128)(2,1)S(1)} %copy-done, bf16[256,2048]{1,0:T(8,128)(2,1)S(1)} %copy-done.1, bf16[256,2048]{1,0:T(8,128)(2,1)S(1)} %copy-done.2, s32[16,27]{1,0:T(8,128)S(1)} %copy-done.3, s32[512]{0:T(512)S(1)} %copy-done.4), custom_call_target="tpu_custom_call" | custom-call | tf_op jit(solution)/shard_map/tile_attention/pallas_call | solution.py:293
  117.7 1.0 copy.7
Async XLA Ops:
  0.0 1.2 %copy-start = (bf16[256,2048]{1,0:T(8,128)(2,1)S(1)}, bf16[256,2048]{1,0:T(8,128)(2,1)}, u32[]{:S(2)}) copy-start(bf16[256,2048]{1,0:T(8,128)(2,1)} %q_ref.1) | copy-start | bytes 3145732
  1.2 1.2 %copy-start.1 = (bf16[256,2048]{1,0:T(8,128)(2,1)S(1)}, bf16[256,2048]{1,0:T(8,128)(2,1)}, u32[]{:S(2)}) copy-start(bf16[256,2048]{1,0:T(8,128)(2,1)} %k_ref.1) | copy-start | bytes 3145732
  2.5 1.2 %copy-start.2 = (bf16[256,2048]{1,0:T(8,128)(2,1)S(1)}, bf16[256,2048]{1,0:T(8,128)(2,1)}, u32[]{:S(2)}) copy-start(bf16[256,2048]{1,0:T(8,128)(2,1)} %v_ref.1) | copy-start | bytes 3145732
  3.7 0.7 copy-start.3
  4.4 0.7 copy-start.4

commit v2 on v1

--- a/solution.py
+++ b/solution.py
@@ -14,7 +14,9 @@
 TL = 16
 PEERS = 16
 ROWS = 256
+PART = 5
 SCALE = math.log2(math.e) / math.sqrt(DIM)
+KFAR, QFAR = True, False
 MESH = pl.DeviceIdType.MESH
 
 
@@ -60,13 +62,18 @@
 
     sign = 1 - 2 * core
 
-    def dest_head(i, side):
-        z = rem(my_z + side * spread(div(i, 2)) + 8, 8)
+    def dest_head(i, side, far):
+        k = div(i, 2)
+        z = rem(my_z + side * spread(7 - k if far else k) + 8, 8)
         return 2 * z + rem(i, 2)
 
-    def source_slot(i):
+    apart = rem(rem(div(pair, 2), 2) + zl, 2)
+    turn = apart * (2 * zl - 1) + (1 - apart) * sign
+
+    def source_slot(i, far):
         r = rem(i, 4)
-        z = rem(zh + sign * spread(div(i, 4)) + 4, 4)
+        k = div(i, 4)
+        z = rem(zh + turn * spread(3 - k if far else k) + 4, 4)
         return rem(r, 2) * 8 + z * 2 + div(r, 2)
 
     def source_dev(slot):
@@ -111,8 +118,8 @@
             pltpu.make_async_copy(src, dst_ref, in_recv.at[a, my_slot]).start()
 
     def sends(i, carry):
-        send(0, k_ref, kraw.at[8 + my_slot], dest_head(i, sign))
-        send(1, v_ref, vraw.at[8 + my_slot], dest_head(i, -sign))
+        send(0, k_ref, kraw.at[8 + my_slot], dest_head(i, sign, KFAR))
+        send(1, v_ref, vraw.at[8 + my_slot], dest_head(i, -sign, KFAR))
         return carry
 
     def window_send(b, start):
@@ -143,6 +150,7 @@
     lax.fori_loop(0, PEERS, sends, 0)
 
     first_tile = (2 * pair - 1) * TL
+    slots = lax.broadcasted_iota(jnp.int32, (16, TILE), 1)
     row_ids = lax.broadcasted_iota(jnp.int32, (TILE, DIM), 0)
 
     def prepare(r):
@@ -152,8 +160,8 @@
             k = kraw[r, u * TILE : (u + 1) * TILE, :].astype(jnp.float32)
             keys[2 * r + u] = jnp.where(usable, k, k[0:1, :]).astype(jnp.bfloat16)
             v = vraw[r, u * TILE : (u + 1) * TILE, :].astype(jnp.float32)
-            vals[2 * r + u, :, 0:DIM] = jnp.where(usable, v, 0.0).astype(jnp.bfloat16)
-            vals[2 * r + u, :, DIM : 2 * DIM] = jnp.where(usable, 1.0, 0.0).astype(jnp.bfloat16)
+            vals[2 * r + u, 0:DIM, :] = jnp.where(usable, v, 0.0).T.astype(jnp.bfloat16)
+            vals[2 * r + u, DIM:, :] = jnp.where(slots < count, 1.0, 0.0).astype(jnp.bfloat16)
 
     def halo(a, raw, slot, dev, there):
         return pltpu.make_async_remote_copy(
@@ -162,7 +170,7 @@
         )
 
     def arrivals(i, carry):
-        slot = source_slot(i)
+        slot = source_slot(i, KFAR)
         for a, raw in ((0, kraw), (1, vraw)):
             here = raw.at[8 + slot]
             pltpu.make_async_copy(here, here, in_recv.at[a, slot]).wait()
@@ -175,25 +183,13 @@
             def _():
                 halo(a, raw, slot, right, rem(slot, 8)).start()
 
-        send(2, q_ref, qbuf.at[my_slot], dest_head(i, sign))
+
+        @pl.when(i >= 8)
+        def _():
+            for n in range(2):
+                send(2, q_ref, qbuf.at[my_slot], dest_head((i - 8) * 2 + n, sign, QFAR))
+
         prepare(8 + slot)
-        return carry
-
-    counts_copy.wait()
-    lax.fori_loop(0, PEERS, arrivals, 0)
-
-    def halo_arrivals(i, carry):
-        slot = source_slot(i)
-        from_left = slot >= 8
-        r = lax.select(from_left, rem(slot, 8), 24 + rem(slot, 8))
-
-        @pl.when((from_left & has_left) | (jnp.logical_not(from_left) & has_right))
-        def _():
-            for a, raw in ((0, kraw), (1, vraw)):
-                here = raw.at[r]
-                pltpu.make_async_copy(here, here, halo_recv.at[a, slot]).wait()
-            prepare(r)
-
         return carry
 
     for half in range(2):
@@ -202,33 +198,83 @@
     copy = pltpu.make_async_copy(wdst, wsm, local.at[1])
     copy.start()
     copy.wait()
+
+    def place_row(i, carry):
+        half, row = div(i, TL), rem(i, TL)
+        for j in range(WIN):
+            wsm[half, row, j] = jnp.clip(wsm[half, row, j] - first_tile, 0, 4 * TL - 1)
+        return carry
+
+    lax.fori_loop(0, 2 * TL, place_row, 0)
+    counts_copy.wait()
+    lax.fori_loop(0, PEERS, arrivals, 0)
+
+    def halo_arrivals(i, carry):
+        slot = source_slot(i, KFAR)
+        from_left = slot >= 8
+        r = lax.select(from_left, rem(slot, 8), 24 + rem(slot, 8))
+
+        @pl.when((from_left & has_left) | (jnp.logical_not(from_left) & has_right))
+        def _():
+            for a, raw in ((0, kraw), (1, vraw)):
+                here = raw.at[r]
+                pltpu.make_async_copy(here, here, halo_recv.at[a, slot]).wait()
+            prepare(r)
+
+        return carry
+
     lax.fori_loop(0, PEERS, halo_arrivals, 0)
 
-    def attend(slot, u):
-        q = qbuf[slot, u * TILE : (u + 1) * TILE, :]
-        half, row = div(slot, 8), 2 * rem(slot, 8) + u
-        at = [jnp.clip(wsm[half, row, j] - first_tile, 0, 4 * TL - 1) for j in range(WIN)]
-        highest = None
-        for j in range(0, WIN, 2):
-            k = keys[at[j]]
-            if j + 1 < WIN:
-                k = jnp.concatenate([k, keys[at[j + 1]]], axis=0)
-            s = lax.dot_general(q, k, (((1,), (1,)), ((), ())), preferred_element_type=jnp.float32)
-            scores[u, :, j * TILE : j * TILE + k.shape[0]] = s
-            for part in range(k.shape[0] // TILE):
-                block = s[:, part * TILE : (part + 1) * TILE]
-                highest = block if highest is None else jnp.maximum(highest, block)
-        highest = jnp.max(highest, axis=1, keepdims=True)
-        total = jnp.zeros((TILE, 2 * DIM), jnp.float32)
-        for j in range(0, WIN, 2):
-            v = vals[at[j]]
-            if j + 1 < WIN:
-                v = jnp.concatenate([v, vals[at[j + 1]]], axis=0)
-            s = scores[u, :, j * TILE : j * TILE + v.shape[0]]
-            weights = jnp.exp2((s - highest) * SCALE).astype(jnp.bfloat16)
-            total += jnp.dot(weights, v, preferred_element_type=jnp.float32)
-        result = total[:, :DIM] / total[:, DIM:]
-        obuf[slot, u * TILE : (u + 1) * TILE, :] = result.astype(jnp.bfloat16)
+    def places(slot):
+        half, row = div(slot, 8), 2 * rem(slot, 8)
+        return [[wsm[half, row + u, j] for j in range(WIN)] for u in range(2)]
+
+    def both(slot):
+        q = [qbuf[slot, u * TILE : (u + 1) * TILE, :] for u in range(2)]
+        none = jnp.zeros_like(q[0])
+        return jnp.concatenate(
+            [jnp.concatenate([q[0], none], axis=1), jnp.concatenate([none, q[1]], axis=1)], axis=0
+        )
+
+    def score_part(j, queries, at, b, highest):
+        n = min(PART, WIN - j)
+        k = jnp.concatenate(
+            [jnp.concatenate([keys[at[0][j + i]], keys[at[1][j + i]]], axis=1) for i in range(n)], axis=0
+        )
+        s = lax.dot_general(k, queries, (((1,), (1,)), ((), ())), preferred_element_type=jnp.float32)
+        scores[b, j * TILE : (j + n) * TILE, :] = s
+        part = jnp.max(s.reshape(n * TILE // 8, 8, 2 * TILE), axis=0)
+        return part if highest is None else jnp.maximum(highest, part)
+
+    def value_part(j, u, at, b, highest, total):
+        n = min(2, WIN - j)
+        v = [vals[at[u][j + i]] for i in range(n)]
+        v = v[0] if n == 1 else jnp.concatenate(v, axis=1)
+        columns = slice(u * TILE, (u + 1) * TILE)
+        s = scores[b, j * TILE : (j + n) * TILE, columns]
+        weights = jnp.exp2((s - highest[:, columns]) * SCALE).astype(jnp.bfloat16)
+        part = jnp.dot(v, weights, preferred_element_type=jnp.float32)
+        return part if total is None else total + part
+
+    def stage(now, then, b, highest):
+        at_now, at_then = places(now), places(then)
+        queries = both(then)
+        parts = list(range(0, WIN, PART))
+        steps = [(u, j) for u in range(2) for j in range(0, WIN, 2)]
+        coming, done = None, 0
+        for step, (u, j) in enumerate(steps):
+            if done < len(parts) and done * len(steps) <= step * len(parts):
+                coming = score_part(parts[done], queries, at_then, 1 - b, coming)
+                done += 1
+            total = value_part(j, u, at_now, b, highest, total if j else None)
+            if j + 2 > WIN:
+                result = total[:DIM] / total[DIM : DIM + 1]
+                obuf[now, u * TILE : (u + 1) * TILE, :] = result.T.astype(jnp.bfloat16)
+        return jnp.max(coming, axis=0, keepdims=True)
+
+    def query_arrival(slot):
+        here = qbuf.at[slot]
+        pltpu.make_async_copy(here, here, in_recv.at[2, slot]).wait()
 
     columns = pl.ds(pl.multiple_of(head * DIM, DIM), DIM)
 
@@ -238,12 +284,16 @@
             recv_sem=o_recv.at[head], device_id=dev, device_id_type=MESH,
         )
 
-    def compute(i, carry):
-        slot = source_slot(i)
-        here = qbuf.at[slot]
-        pltpu.make_async_copy(here, here, in_recv.at[2, slot]).wait()
-        for u in range(2):
-            attend(slot, u)
+    def chunk(i, b, highest):
+        slot = source_slot(i, QFAR)
+        later = jnp.minimum(i + 1, PEERS - 1)
+        next_slot = source_slot(later, QFAR)
+
+        @pl.when(later > i)
+        def _():
+            query_arrival(next_slot)
+
+        highest = stage(slot, next_slot, b, highest)
         dev = source_dev(slot)
         mine = is_me(dev)
 
@@ -255,9 +305,19 @@
         def _():
             pltpu.make_async_copy(obuf.at[slot], out_ref.at[:, columns], o_recv.at[head]).start()
 
-        return carry
-
-    lax.fori_loop(0, PEERS, compute, 0)
+        return highest
+
+    def chunks(i, highest):
+        for b in range(2):
+            highest = chunk(2 * i + b, b, highest)
+        return highest
+
+    first = source_slot(jnp.int32(0), QFAR)
+    query_arrival(first)
+    highest = None
+    for j in range(0, WIN, PART):
+        highest = score_part(j, both(first), places(first), 0, highest)
+    lax.fori_loop(0, PEERS // 2, chunks, jnp.max(highest, axis=0, keepdims=True))
 
     def finish(i, carry):
         dst = owner(src_pair, i)
@@ -306,9 +366,9 @@
             pltpu.VMEM((2 * PEERS, ROWS, DIM), jnp.bfloat16),
             pltpu.VMEM((2 * PEERS, ROWS, DIM), jnp.bfloat16),
             pltpu.VMEM((4 * TL, TILE, DIM), jnp.bfloat16),
-            pltpu.VMEM((4 * TL, TILE, 2 * DIM), jnp.bfloat16),
+            pltpu.VMEM((4 * TL, DIM + 16, TILE), jnp.bfloat16),
             pltpu.VMEM((PEERS, ROWS, DIM), jnp.bfloat16),
-            pltpu.VMEM((2, TILE, WIN * TILE), jnp.float32),
+            pltpu.VMEM((2, WIN * TILE, 2 * TILE), jnp.float32),
             pltpu.VMEM((2, TL, WIN), jnp.int32),
             pltpu.SMEM((2, TL, WIN), jnp.int32),
             pltpu.SMEM((32 * TL,), jnp.int32),
@@ -323,7 +383,7 @@
             dma((2,)),
         ],
         compiler_params=pltpu.CompilerParams(
-            collective_id=0, has_side_effects=True, vmem_limit_bytes=48 * 1024 * 1024
+            collective_id=0, has_side_effects=True, vmem_limit_bytes=60 * 1024 * 1024
         ),
         name="tile_attention",
     )(queries, keys, values, windows, counts)

time: 121 us -> 115 us (0.950); the launches traced: 119 us -> 115 us
  local copies, waits for them, and re-layouts: 6.02 us -> 2.3 us
    unnamed x11 -> x1, local copies, waits for them, and re-layouts: 6.02 us -> 2.3 us
where the time goes in v2:
time: 115 us
  Pallas kernels  113 us (98%)
  local copies, waits for them, and re-layouts  2.3 us (2%)
    pallas_call x1, Pallas kernels, shards(): pl.pallas_call(kernel, out_shape=jax.ShapeDtypeStruct(queries.shape, jnp....  113 us
    unnamed x1, local copies, waits for them, and re-layouts  2.3 us

profile of v2, /device:TPU:57, one launch (start us, length us, event | category | flops | bytes accessed | tf_op | source)
XLA Modules:
  0.0 115.1 jit_solution(12016995022078765804)
XLA Ops:
  0.0 112.8 %tile_attention.1 = bf16[256,2048]{1,0:T(8,128)(2,1)} custom-call(bf16[256,2048]{1,0:T(8,128)(2,1)} %q_ref.1, bf16[256,2048]{1,0:T(8,128)(2,1)} %k_ref.1, bf16[256,2048]{1,0:T(8,128)(2,1)} %v_ref.1, s32[16,27]{1,0:T(8,128)} %win_ref.1, s32[512]{0:T(512)} %counts_hbm.1), custom_call_target="tpu_custom_call" | custom-call | tf_op jit(solution)/shard_map/tile_attention/pallas_call | solution.py:353
  112.8 2.3 %copy.7 = bf16[256,2048]{1,0:T(8,128)(2,1)} copy(bf16[256,2048]{1,0:T(8,128)(2,1)} %tile_attention.1) | data formatting | bytes 2097152

commit v3 on v2

--- a/solution.py
+++ b/solution.py
@@ -74,7 +74,7 @@
         r = rem(i, 4)
         k = div(i, 4)
         z = rem(zh + turn * spread(3 - k if far else k) + 4, 4)
-        return rem(r, 2) * 8 + z * 2 + div(r, 2)
+        return rem(r, 2) * 8 + z * 2 + rem(div(r, 2) + core + zl, 2)
 
     def source_dev(slot):
         return 2 * pair + div(slot, 8), rem(slot, 8)
@@ -284,6 +284,21 @@
             recv_sem=o_recv.at[head], device_id=dev, device_id_type=MESH,
         )
 
+    def sent(i):
+        h = dest_head(i, sign, QFAR)
+
+        @pl.when(jnp.logical_not(is_me(owner(src_pair, h))))
+        def _():
+            for a, ref in ((0, k_ref), (1, v_ref), (2, q_ref)):
+                src = ref.at[:, pl.ds(pl.multiple_of(h * DIM, DIM), DIM)]
+                pltpu.make_async_copy(src, src, in_send.at[a, h]).wait()
+
+        @pl.when(((i < 8) & has_left) | ((i >= 8) & has_right))
+        def _():
+            for a, raw in ((0, kraw), (1, vraw)):
+                there = raw.at[8 + i]
+                pltpu.make_async_copy(there, there, halo_send.at[a, i]).wait()
+
     def chunk(i, b, highest):
         slot = source_slot(i, QFAR)
         later = jnp.minimum(i + 1, PEERS - 1)
@@ -305,6 +320,7 @@
         def _():
             pltpu.make_async_copy(obuf.at[slot], out_ref.at[:, columns], o_recv.at[head]).start()
 
+        sent(i)
         return highest
 
     def chunks(i, highest):
@@ -320,20 +336,6 @@
     lax.fori_loop(0, PEERS // 2, chunks, jnp.max(highest, axis=0, keepdims=True))
 
     def finish(i, carry):
-        dst = owner(src_pair, i)
-
-        @pl.when(jnp.logical_not(is_me(dst)))
-        def _():
-            for a, ref in ((0, k_ref), (1, v_ref), (2, q_ref)):
-                src = ref.at[:, pl.ds(pl.multiple_of(i * DIM, DIM), DIM)]
-                pltpu.make_async_copy(src, src, in_send.at[a, i]).wait()
-
-        @pl.when(((i < 8) & has_left) | ((i >= 8) & has_right))
-        def _():
-            for a, raw in ((0, kraw), (1, vraw)):
-                there = raw.at[8 + i]
-                pltpu.make_async_copy(there, there, halo_send.at[a, i]).wait()
-
         @pl.when(jnp.logical_not(is_me(source_dev(i))))
         def _():
             pltpu.make_async_copy(obuf.at[i], obuf.at[i], o_send.at[i]).wait()
@@ -352,7 +354,7 @@
     dma = pltpu.SemaphoreType.DMA
     return pl.pallas_call(
         kernel,
-        out_shape=jax.ShapeDtypeStruct(queries.shape, jnp.bfloat16),
+        out_shape=pltpu.VMEM(queries.shape, jnp.bfloat16),
         in_specs=[
             anywhere,
             anywhere,
@@ -360,7 +362,7 @@
             anywhere,
             anywhere,
         ],
-        out_specs=anywhere,
+        out_specs=pl.BlockSpec(memory_space=pltpu.VMEM),
         scratch_shapes=[
             pltpu.VMEM((PEERS, ROWS, DIM), jnp.bfloat16),
             pltpu.VMEM((2 * PEERS, ROWS, DIM), jnp.bfloat16),

time: 115 us -> 113 us (0.983)
  local copies, waits for them, and re-layouts: 2.3 us -> 0.97 us
    unnamed x1, local copies, waits for them, and re-layouts: 2.3 us -> 0.97 us
where the time goes in v3:
time: 113 us
  Pallas kernels  112 us (99%)
    pallas_call x1, Pallas kernels, shards(): pl.pallas_call(kernel, out_shape=pltpu.VMEM(queries.shape, jnp.bfloat16),...  112 us

profile of v3, /device:TPU:57, one launch (start us, length us, event | category | flops | bytes accessed | tf_op | source)
XLA Modules:
  0.0 113.1 jit_solution(7390028404063514805)
XLA Ops:
  0.0 112.1 %tile_attention.1 = bf16[256,2048]{1,0:T(8,128)(2,1)S(1)} custom-call(bf16[256,2048]{1,0:T(8,128)(2,1)} %q_ref.1, bf16[256,2048]{1,0:T(8,128)(2,1)} %k_ref.1, bf16[256,2048]{1,0:T(8,128)(2,1)} %v_ref.1, s32[16,27]{1,0:T(8,128)} %win_ref.1, s32[512]{0:T(512)} %counts_hbm.1), custom_call_target="tpu_custom_call" | custom-call | tf_op jit(solution)/shard_map/tile_attention/pallas_call | solution.py:355
  112.1 1.0 copy.7

commit v4 on v3

--- a/solution.py
+++ b/solution.py
@@ -118,8 +118,8 @@
             pltpu.make_async_copy(src, dst_ref, in_recv.at[a, my_slot]).start()
 
     def sends(i, carry):
-        send(0, k_ref, kraw.at[8 + my_slot], dest_head(i, sign, KFAR))
-        send(1, v_ref, vraw.at[8 + my_slot], dest_head(i, -sign, KFAR))
+        send(0, k_ref, kraw.at[8 + my_slot], dest_head(rem(i + 8 * core, 16), sign, KFAR))
+        send(1, v_ref, vraw.at[8 + my_slot], dest_head(rem(i + 8 * core, 16), -sign, KFAR))
         return carry
 
     def window_send(b, start):

time: 113 us -> 112 us (level); the launches traced: 113 us -> 111 us
  Pallas kernels: 112 us -> 110 us
    pallas_call x1, Pallas kernels: 112 us -> 110 us  [shards(): pl.pallas_call(kernel, out_shape=pltpu.VMEM(queries.shape, jnp.bfloat16),...]
where the time goes in v4:
time: 112 us; the launch traced here: 111 us
  Pallas kernels  110 us (98%)
    pallas_call x1, Pallas kernels, shards(): pl.pallas_call(kernel, out_shape=pltpu.VMEM(queries.shape, jnp.bfloat16),...  110 us

profile of v4, /device:TPU:57, one launch (start us, length us, event | category | flops | bytes accessed | tf_op | source)
XLA Modules:
  0.0 110.7 jit_solution(9803432062892543728)
XLA Ops:
  0.0 109.7 %tile_attention.1 = bf16[256,2048]{1,0:T(8,128)(2,1)S(1)} custom-call(bf16[256,2048]{1,0:T(8,128)(2,1)} %q_ref.1, bf16[256,2048]{1,0:T(8,128)(2,1)} %k_ref.1, bf16[256,2048]{1,0:T(8,128)(2,1)} %v_ref.1, s32[16,27]{1,0:T(8,128)} %win_ref.1, s32[512]{0:T(512)} %counts_hbm.1), custom_call_target="tpu_custom_call" | custom-call | tf_op jit(solution)/shard_map/tile_attention/pallas_call | solution.py:355
  109.7 1.0 copy.7
